TPU v7x, 32 devices: a whole 2x2x4 slice. The times are simulated.
32 devices in a mesh: node: 4 (over y, core), local: 8 (over z, x).
Axes of the slice: x: 2, y: 2, z: 4, core: 2. Of those that a mesh axis runs over, the one named last changes fastest.
Arguments:
- tokens: bfloat16 [2048, 3584], P(('node', 'local')), may hold values from -6 to 6
- expert_ids: int32 [2048, 8], P(('node', 'local')), may hold values from 0 to 31, as said below
- gate_values: bfloat16 [2048, 8], P(('node', 'local')), may hold values from 0.049804688 to 0.44921875
- expert_gate: bfloat16 [32, 3584, 1024], P(('node', 'local')), may hold values from -0.09375 to 0.09375
- expert_up: bfloat16 [32, 3584, 1024], P(('node', 'local')), may hold values from -0.09375 to 0.09375
- expert_down: bfloat16 [32, 1024, 3584], P(('node', 'local')), may hold values from -0.1875 to 0.1875
Outputs:
- mixed: bfloat16 [2048, 3584], P(('node', 'local'))
Inputs may be any that keep to these rules, and one draw needn't show every extreme that they name: `expert_ids`: each row names 8 different experts, the same number on each of exactly 4 nodes. Among the rows of one device, each node is named by exactly 64 rows, no expert is named more than 32 times, and on every node some expert is named exactly 32 times.
All inputs are finite; a program needn't handle non-finite values.
Results may differ from a plain program's by a relative error of at most 0.012.
Values may be sent and summed in bfloat16 or wider, within the bound.
A program may use at most 128 MiB of HBM per device.

v0:
```python
import jax
import jax.numpy as jnp
from jax import lax
from jax.sharding import PartitionSpec as P


def expert_rows(rows, w_gate, w_up, w_down):
    shape = rows.shape
    flat = rows.reshape(-1, shape[-1])
    gate_rows = jnp.dot(flat, w_gate, preferred_element_type=jnp.float32)
    up_rows = jnp.dot(flat, w_up, preferred_element_type=jnp.float32)
    hidden = (jax.nn.silu(gate_rows) * up_rows).astype(jnp.bfloat16)
    output = jnp.dot(hidden, w_down, preferred_element_type=jnp.float32).astype(jnp.bfloat16)
    return output.reshape(shape)


def shards(tokens, expert_ids, gate_values, expert_gate, expert_up, expert_down):
    nodes = lax.axis_size("node")
    per_node = lax.axis_size("local")
    experts = nodes * per_node
    tok_rows, width = tokens.shape
    top = expert_ids.shape[1]
    cap = 2 * tok_rows * top // experts
    w_gate = expert_gate[0]
    w_up = expert_up[0]
    w_down = expert_down[0]
    hits = (expert_ids[:, :, None] == jnp.arange(experts, dtype=jnp.int32)[None, None, :]).astype(
        jnp.int32
    )
    flat_hits = hits.reshape(tok_rows * top, experts)
    earlier = jnp.cumsum(flat_hits, axis=0) - flat_hits
    slot = jnp.sum(earlier * flat_hits, axis=1).reshape(tok_rows, top)
    position = expert_ids * cap + slot
    places = jnp.arange(experts * cap, dtype=jnp.int32)
    chosen = places[:, None, None] == position[None, :, :]
    dispatch = jnp.any(chosen, axis=2).astype(jnp.bfloat16)
    weights = jnp.sum(
        jnp.where(chosen, gate_values[None, :, :].astype(jnp.float32), jnp.float32(0.0)), axis=2
    )
    send = jnp.dot(dispatch, tokens, preferred_element_type=jnp.float32).astype(jnp.bfloat16)
    back = lax.all_to_all(
        expert_rows(
            lax.all_to_all(
                send.reshape(experts, cap, width),
                ("node", "local"),
                split_axis=0,
                concat_axis=0,
                tiled=True,
            ),
            w_gate,
            w_up,
            w_down,
        ),
        ("node", "local"),
        split_axis=0,
        concat_axis=0,
        tiled=True,
    )
    mix = weights.astype(jnp.bfloat16).reshape(nodes, per_node * cap, tok_rows)
    node_part = jnp.einsum(
        "nct,ncd->ntd",
        mix,
        back.reshape(nodes, per_node * cap, width),
        preferred_element_type=jnp.float32,
    ).astype(jnp.bfloat16)
    return jnp.sum(node_part.astype(jnp.float32), axis=0).astype(jnp.bfloat16)


def solution(mesh):
    placed = (
        P(("node", "local"), None),
        P(("node", "local"), None),
        P(("node", "local"), None),
        P(("node", "local"), None, None),
        P(("node", "local"), None, None),
        P(("node", "local"), None, None),
    )
    return jax.shard_map(
        shards, mesh=mesh, in_specs=placed, out_specs=P(("node", "local"), None), check_vma=False
    )
```

profile of v0, /device:TPU:0, one launch (start us, length us, event | category | flops | bytes accessed | tf_op | source)
XLA Modules:
  0.0 377.3 jit_solution(11570262474906971319)
XLA Ops:
  0.0 0.0 copy-start
  0.0 0.8 copy.23
  0.8 0.1 eq.44
  0.9 0.1 eq.40
  1.0 1.2 reduce-window.6
  2.2 0.2 slice_reduce_fusion
  2.5 0.1 fusion.13
  2.6 0.1 reshape.40
  2.7 0.1 copy.26
  2.7 0.7 multiply_add_fusion
  3.4 0.1 copy.27
  3.5 0.7 fusion.7
  4.2 0.0 copy-done
  4.2 0.0 slice-start
  4.2 2.1 convolution_convert_fusion.1
  6.4 0.0 slice-start.1
  6.4 0.0 slice-start.2
  6.4 169.5 %all_to_all.10 = bf16[32,32,3584]{2,1,0:T(8,128)(2,1)S(1)} all-to-all(bf16[32,32,3584]{2,1,0:T(8,128)(2,1)S(1)} %bitcast.44), channel_id=1, replica_groups=mesh['node'=4,'local'=8] {'node','local'}, dimensions={0} | all-to-all | bytes 14680064 | tf_op jit(solution)/shard_map/all_to_all | solution.py:43
  175.9 0.0 slice-done
  175.9 0.0 slice-done.1
  175.9 0.0 slice-start.3
  175.9 0.0 slice-start.4
  175.9 9.3 %fusion.1 = f32[1024,1024]{1,0:T(8,128)} fusion(bf16[1024,3584]{1,0:T(8,128)(2,1)S(1)} %bitcast.46, bf16[1,3584,1024]{2,1,0:T(8,128)(2,1)S(1)} %bitcast.50), kind=kOutput, calls=%fused_computation.3 | convolution fusion | flops 7516192768 | bytes 18874368 | tf_op jit(solution)/shard_map/dot_general | solution.py:11
  185.2 0.0 slice-done.2
  185.2 0.0 slice-done.3
  185.2 0.0 slice-start.5
  185.2 10.3 %multiply_convert_fusion = bf16[1024,1024]{1,0:T(8,128)(2,1)S(1)} fusion(f32[1024,1024]{1,0:T(8,128)} %fusion.1, bf16[1024,3584]{1,0:T(8,128)(2,1)S(1)} %bitcast.47, bf16[1,3584,1024]{2,1,0:T(8,128)(2,1)S(1)} %bitcast.52), kind=kOutput, calls=%fused_computation.8 | convolution fusion | flops 7522484224 | bytes 20971520 | tf_op jit(solution)/shard_map/dot_general | solution.py:10
  195.5 0.0 slice-done.4
  195.5 0.0 slice-done.5
  195.5 9.7 %convolution_convert_fusion = bf16[1024,3584]{1,0:T(8,128)(2,1)} fusion(bf16[1024,1024]{1,0:T(8,128)(2,1)S(1)} %multiply_convert_fusion, bf16[1,1024,3584]{2,1,0:T(8,128)(2,1)S(1)} %bitcast.54), kind=kOutput, calls=%fused_computation | convolution fusion | flops 7519862784 | bytes 16777216 | tf_op jit(solution)/shard_map/dot_general | solution.py:13
  205.2 0.0 copy-start.1
  205.2 3.8 all-to-all-start.1
  209.0 0.0 copy-done.1
  209.0 0.1 copy.28
  209.1 0.7 select_reduce_fusion
  209.8 162.1 %all-to-all-done.1 = bf16[32,32,3584]{2,1,0:T(8,128)(2,1)} async-done(((bf16[32,32,3584]{2,1,0:T(8,128)(2,1)}), bf16[32,32,3584]{2,1,0:T(8,128)(2,1)}, u32[]{:S(2)}, u32[]{:S(2)}) %all-to-all-start.1) | async-done | bytes 7340064 | tf_op jit(solution)/shard_map/all_to_all | solution.py:41
  371.9 5.3 %fusion.8 = bf16[64,3584]{1,0:T(8,128)(2,1)} fusion(bf16[4,256,3584]{2,1,0:T(8,128)(2,1)} %bitcast.7, bf16[8,4,8,256]{3,2,1,0:T(8,128)(2,1)S(1)} %bitcast.48), kind=kOutput, calls=%fused_computation.12 | convolution fusion | flops 471367680 | bytes 7929856 | tf_op jit(solution)/shard_map/nct,ncd->ntd/dot_general | solution.py:60
  (6 shorter events, 0.0 us)
Async XLA Ops:
  0.0 4.2 %copy-start = (bf16[64,3584]{1,0:T(8,128)(2,1)S(1)}, bf16[64,3584]{1,0:T(8,128)(2,1)}, u32[]{:S(2)}) copy-start(bf16[64,3584]{1,0:T(8,128)(2,1)} %param.6) | copy-start | bytes 1376260
  4.2 171.7 %slice-start = ((s8[7340032]{0:T(1024)(128)(4,1)}), s8[4194304]{0:T(1024)(128)(4,1)S(1)}, s32[]{:S(2)}) async-start(s8[7340032]{0:T(1024)(128)(4,1)} %bitcast.49), calls=%async_computation.2 | async-start | bytes 8388608
  6.4 169.6 %slice-start.1 = ((s8[7340032]{0:T(1024)(128)(4,1)}), s8[3145728]{0:T(1024)(128)(4,1)S(1)}, s32[]{:S(2)}) async-start(s8[7340032]{0:T(1024)(128)(4,1)} %bitcast.49), calls=%async_computation.3 | async-start | bytes 6291456
  6.4 178.8 %slice-start.2 = ((s8[7340032]{0:T(1024)(128)(4,1)}), s8[4194304]{0:T(1024)(128)(4,1)S(1)}, s32[]{:S(2)}) async-start(s8[7340032]{0:T(1024)(128)(4,1)} %bitcast.51), calls=%async_computation.4 | async-start | bytes 8388608
  175.9 9.3 %slice-start.3 = ((s8[7340032]{0:T(1024)(128)(4,1)}), s8[3145728]{0:T(1024)(128)(4,1)S(1)}, s32[]{:S(2)}) async-start(s8[7340032]{0:T(1024)(128)(4,1)} %bitcast.51), calls=%async_computation.5 | async-start | bytes 6291456
  175.9 19.6 %slice-start.4 = ((s8[7340032]{0:T(1024)(128)(4,1)}), s8[4194304]{0:T(1024)(128)(4,1)S(1)}, s32[]{:S(2)}) async-start(s8[7340032]{0:T(1024)(128)(4,1)} %bitcast.53), calls=%async_computation.6 | async-start | bytes 8388608
  185.2 10.3 %slice-start.5 = ((s8[7340032]{0:T(1024)(128)(4,1)}), s8[3145728]{0:T(1024)(128)(4,1)S(1)}, s32[]{:S(2)}) async-start(s8[7340032]{0:T(1024)(128)(4,1)} %bitcast.53), calls=%async_computation.7 | async-start | bytes 6291456
  205.2 3.8 copy-start.1
  205.2 166.7 %all-to-all-start.1 = ((bf16[32,32,3584]{2,1,0:T(8,128)(2,1)}), bf16[32,32,3584]{2,1,0:T(8,128)(2,1)}, u32[]{:S(2)}, u32[]{:S(2)}) async-start(bf16[32,32,3584]{2,1,0:T(8,128)(2,1)} %bitcast.45), calls=%async_computation.1 | async-start | bytes 14680064 | tf_op jit(solution)/shard_map/all_to_all | solution.py:41
where the time goes:
time: 378 us; the launch traced here: 377 us
  blocking collectives  170 us (45%)
  waiting for transfers between devices  162 us (43%)
  matrix products  36.7 us (10%)
    all_to_all x1, blocking collectives, shards(): lax.all_to_all(send.reshape(experts, cap, width), ('node', 'local'), spli...  170 us
    all_to_all x1, waiting for transfers between devices, shards(): lax.all_to_all(expert_rows(lax.all_to_all(send.reshape(experts, cap, widt...  162 us
    dot_general x1, matrix products, expert_rows(): gate_rows = jnp.dot(flat, w_gate, preferred_element_type=jnp.float32)  10.3 us
    dot_general x1, matrix products, expert_rows(): jnp.dot(hidden, w_down, preferred_element_type=jnp.float32)  9.72 us
    dot_general x1, matrix products, expert_rows(): up_rows = jnp.dot(flat, w_up, preferred_element_type=jnp.float32)  9.27 us
  transfers between devices with their start and end apart: 1, of which 1 were waited for; matrix products, arithmetic and copies ran while one was open for 0% of the time, Pallas kernels for 0%

commit v1 on v0

--- a/solution.py
+++ b/solution.py
@@ -1,7 +1,15 @@
+import functools
+
 import jax
 import jax.numpy as jnp
 from jax import lax
+from jax.experimental import pallas as pl
+from jax.experimental.pallas import tpu as pltpu
 from jax.sharding import PartitionSpec as P
+
+BF16 = jnp.bfloat16
+F32 = jnp.float32
+LANES = 128
 
 
 def expert_rows(rows, w_gate, w_up, w_down):
@@ -14,7 +22,7 @@
     return output.reshape(shape)
 
 
-def shards(tokens, expert_ids, gate_values, expert_gate, expert_up, expert_down):
+def shards_all_to_all(tokens, expert_ids, gate_values, expert_gate, expert_up, expert_down):
     nodes = lax.axis_size("node")
     per_node = lax.axis_size("local")
     experts = nodes * per_node
@@ -66,6 +74,427 @@
     return jnp.sum(node_part.astype(jnp.float32), axis=0).astype(jnp.bfloat16)
 
 
+def fused(
+    spots,
+    experts,
+    cap,
+    tok_ref,
+    ids_ref,
+    gates_ref,
+    gate_hbm,
+    up_hbm,
+    down_hbm,
+    out_ref,
+    held,
+    mine,
+    from_core,
+    from_second,
+    from_first,
+    from_line,
+    w_gate,
+    w_up,
+    w_down,
+    rows,
+    hidden,
+    pick,
+    blend,
+    local_sem,
+    line_s,
+    line_r,
+    first_s,
+    first_r,
+    second_s,
+    second_r,
+    core_s,
+    core_r,
+    back_core_s,
+    back_core_r,
+    back_second_s,
+    back_second_r,
+    back_first_s,
+    back_first_r,
+    back_line_s,
+    back_line_r,
+):
+    tok_rows, width = tok_ref.shape
+    ff = w_gate.shape[1]
+    quad = 4 * tok_rows
+    slots = 4 * cap
+    node = lax.axis_index("node")
+    local = lax.axis_index("local")
+    expert = node * (2 * spots) + local
+    y, c, z, x = node // 2, node % 2, local // 2, local % 2
+    a, b = x + c * (y - x), y + c * (x - y)
+    step_a, step_b = 1 + c, 2 - c
+
+    def q(i, j):
+        return i * step_a + j * step_b
+
+    def q_core(i, j):
+        return i * step_b + j * step_a
+
+    own = q(a, b)
+    order = ((a, b), (1 - a, b), (a, 1 - b), (1 - a, 1 - b))
+    order_core = ((b, a), (1 - b, a), (b, 1 - a), (1 - b, 1 - a))
+    first = ((y + c * (1 - 2 * y)) * 2 + c, z * 2 + x + (1 - c) * (1 - 2 * x))
+    second = ((y + (1 - c) * (1 - 2 * y)) * 2 + c, z * 2 + x + c * (1 - 2 * x))
+    sibling = (y * 2 + 1 - c, local)
+
+    def along(k):
+        return (node, ((z + k) % spots) * 2 + x)
+
+    def spot(k):
+        return (z + spots - k) % spots
+
+    barrier = pltpu.get_barrier_semaphore()
+    partners = [first, second, sibling] + [along(k) for k in range(1, spots)]
+    for partner in partners:
+        pl.semaphore_signal(
+            barrier, inc=1, device_id=partner, device_id_type=pl.DeviceIdType.MESH
+        )
+
+    loads = [
+        pltpu.make_async_copy(tok_ref, mine.at[:, pl.ds(0, width)], local_sem.at[0]),
+        pltpu.make_async_copy(gate_hbm.at[0], w_gate, local_sem.at[1]),
+        pltpu.make_async_copy(up_hbm.at[0], w_up, local_sem.at[2]),
+        pltpu.make_async_copy(down_hbm.at[0], w_down, local_sem.at[3]),
+    ]
+    for load in loads:
+        load.start()
+
+    lane = lax.broadcasted_iota(jnp.int32, (tok_rows, LANES), 1)
+    weight = jnp.zeros((tok_rows, LANES), F32)
+    hit = jnp.zeros((tok_rows, LANES), F32)
+    for k in range(ids_ref.shape[1]):
+        chosen = ids_ref[:, k : k + 1]
+        value = gates_ref[:, k : k + 1].astype(F32)
+        weight = weight + jnp.where(lane == chosen, value, 0.0)
+        hit = hit + jnp.where(lane == chosen + experts, 1.0, 0.0)
+    earlier = (
+        lax.broadcasted_iota(jnp.int32, (tok_rows, tok_rows), 0)
+        > lax.broadcasted_iota(jnp.int32, (tok_rows, tok_rows), 1)
+    )
+    before = jnp.dot(
+        jnp.where(earlier, 1.0, 0.0).astype(BF16), hit.astype(BF16), preferred_element_type=F32
+    )
+    mine[:, pl.ds(width, LANES)] = (weight + hit * (before + 1.0)).astype(BF16)
+    loads[0].wait()
+    keep = pltpu.make_async_copy(mine, held.at[z, c, own], local_sem.at[4])
+    keep.start()
+    pl.semaphore_wait(barrier, len(partners))
+
+    def send(src, dst, send_sem, recv_sem, device):
+        return pltpu.make_async_remote_copy(
+            src_ref=src,
+            dst_ref=dst,
+            send_sem=send_sem,
+            recv_sem=recv_sem,
+            device_id=device,
+            device_id_type=pl.DeviceIdType.MESH,
+        )
+
+    def block(k, i):
+        return held.at[spot(k), c, q(*order[i])]
+
+    def source(k, i):
+        return mine if k == 0 and i == 0 else block(k, i)
+
+    def to_line(k):
+        return send(mine, held.at[z, c, own], line_s.at[k - 1], line_r.at[k - 1], along(k))
+
+    def to_first(k):
+        return send(source(k, 0), block(k, 0), first_s.at[k], first_r.at[k], first)
+
+    def to_second(k, i):
+        return send(source(k, i), block(k, i), second_s.at[k, i], second_r.at[k, i], second)
+
+    def to_core(k, i):
+        return send(source(k, i), block(k, i), core_s.at[k, i], core_r.at[k, i], sibling)
+
+    def gather_a(k):
+        if k > 0:
+            send(mine, block(k, 0), line_s.at[k - 1], line_r.at[k - 1], along(k)).wait_recv()
+        to_first(k).start()
+        to_second(k, 0).start()
+        to_core(k, 0).start()
+        if k == 0:
+            for hop in range(1, spots):
+                to_line(hop).start()
+
+    def gather_b(k):
+        send(mine, block(k, 1), first_s.at[k], first_r.at[k], first).wait_recv()
+        to_second(k, 1).start()
+        to_core(k, 1).start()
+
+    def gather_c(k):
+        for i in range(2):
+            send(
+                mine, block(k, 2 + i), second_s.at[k, i], second_r.at[k, i], second
+            ).wait_recv()
+            to_core(k, 2 + i).start()
+
+    def gather_d(k):
+        for i in range(4):
+            place = held.at[spot(k), 1 - c, q_core(*order_core[i])]
+            send(mine, place, core_s.at[k, i], core_r.at[k, i], sibling).wait_recv()
+
+    def gather_sent(k):
+        to_first(k).wait_send()
+        for i in range(2):
+            to_second(k, i).wait_send()
+        for i in range(4):
+            to_core(k, i).wait_send()
+
+    def dispatch(k):
+        s = spot(k)
+        lane = lax.broadcasted_iota(jnp.int32, (quad, LANES), 1)
+        base = (lax.broadcasted_iota(jnp.int32, (quad, 1), 0) // tok_rows * cap).astype(F32)
+        column = lax.broadcasted_iota(jnp.int32, (quad, slots), 1).astype(F32)
+        for h in range(2):
+            notes = held[s, h, :, :, pl.ds(width, LANES)].reshape(quad, LANES).astype(F32)
+            weight = jnp.sum(jnp.where(lane == expert, notes, 0.0), axis=1, keepdims=True)
+            place = jnp.sum(
+                jnp.where(lane == expert + experts, notes, 0.0), axis=1, keepdims=True
+            )
+            target = jnp.where(place > 0.0, place - 1.0 + base, -1.0)
+            pick[h] = jnp.where(column == target, 1.0, 0.0).astype(BF16)
+            blend[h] = jnp.where(column == target, weight, 0.0).astype(BF16)
+
+        def piece(j, carry):
+            cols = pl.ds(pl.multiple_of(j * 512, 512), 512)
+            for h in range(2):
+                rows[pl.ds(h * slots, slots), cols] = lax.dot_general(
+                    pick[h],
+                    held[s, h, :, :, cols].reshape(quad, 512),
+                    (((0,), (0,)), ((), ())),
+                    preferred_element_type=F32,
+                ).astype(BF16)
+            return carry
+
+        lax.fori_loop(0, width // 512, piece, 0)
+
+    def expand(k):
+        if k == 0:
+            loads[1].wait()
+            loads[2].wait()
+
+        def piece(j, carry):
+            cols = pl.ds(pl.multiple_of(j * 256, 256), 256)
+            gate = jnp.dot(rows[...], w_gate[:, cols], preferred_element_type=F32)
+            up = jnp.dot(rows[...], w_up[:, cols], preferred_element_type=F32)
+            hidden[:, cols] = (gate / (1.0 + jnp.exp(-gate)) * up).astype(BF16)
+            return carry
+
+        lax.fori_loop(0, ff // 256, piece, 0)
+
+    def contract(k):
+        s = spot(k)
+        if k == 0:
+            loads[3].wait()
+        gather_sent(k)
+
+        def piece(j, carry):
+            cols = pl.ds(pl.multiple_of(j * 512, 512), 512)
+            made = jnp.dot(hidden[...], w_down[:, cols], preferred_element_type=F32).astype(BF16)
+            for h in range(2):
+                held[s, h, :, :, cols] = (
+                    jnp.dot(
+                        blend[h], made[h * slots : (h + 1) * slots], preferred_element_type=F32
+                    )
+                    .astype(BF16)
+                    .reshape(4, tok_rows, 512)
+                )
+            return carry
+
+        lax.fori_loop(0, width // 512, piece, 0)
+
+    features = pl.ds(0, width)
+
+    def back_core(k):
+        return send(
+            held.at[spot(k), 1 - c, :, :, features],
+            from_core.at[k],
+            back_core_s.at[k],
+            back_core_r.at[k],
+            sibling,
+        )
+
+    def back_second(k, i):
+        return send(
+            held.at[spot(k), c, q(i, 1 - b), :, features],
+            from_second.at[k, i],
+            back_second_s.at[k, i],
+            back_second_r.at[k, i],
+            second,
+        )
+
+    def back_first(k):
+        return send(
+            held.at[spot(k), c, q(1 - a, b), :, features],
+            from_first.at[k],
+            back_first_s.at[k],
+            back_first_r.at[k],
+            first,
+        )
+
+    def back_line(k):
+        return send(
+            held.at[spot(k), c, own, :, features],
+            from_line.at[k - 1],
+            back_line_s.at[k - 1],
+            back_line_r.at[k - 1],
+            (node, spot(k) * 2 + x),
+        )
+
+    def add(k, place, other):
+        held[spot(k), c, place, :, features] = (
+            held[spot(k), c, place, :, features].astype(F32) + other.astype(F32)
+        ).astype(BF16)
+
+    def back_1(k):
+        back_core(k).start()
+
+    def back_2(k):
+        back_core(k).wait_recv()
+        for i in range(2):
+            add(k, q(i, 1 - b), from_core[k, q(i, 1 - b)])
+            back_second(k, i).start()
+        for i in range(2):
+            add(k, q(i, b), from_core[k, q(i, b)])
+
+    def back_3(k):
+        back_second(k, 0).wait_recv()
+        back_second(k, 1).wait_recv()
+        add(k, q(1 - a, b), from_second[k, 1 - a])
+        back_first(k).start()
+        add(k, own, from_second[k, a])
+
+    def back_4(k):
+        back_first(k).wait_recv()
+        add(k, own, from_first[k])
+        if k > 0:
+            back_line(k).start()
+
+    gather_a(0)
+    gather_b(0)
+    gather_a(1)
+    gather_c(0)
+    gather_b(1)
+    gather_d(0)
+    keep.wait()
+    dispatch(0)
+    expand(0)
+    gather_c(1)
+    gather_a(2)
+    contract(0)
+    back_1(0)
+    gather_b(2)
+    gather_d(1)
+    dispatch(1)
+    back_2(0)
+    expand(1)
+    gather_c(2)
+    gather_a(3)
+    contract(1)
+    back_1(1)
+    back_3(0)
+    gather_b(3)
+    gather_d(2)
+    dispatch(2)
+    back_2(1)
+    expand(2)
+    gather_c(3)
+    back_4(0)
+    contract(2)
+    back_1(2)
+    back_3(1)
+    gather_d(3)
+    dispatch(3)
+    back_2(2)
+    expand(3)
+    back_4(1)
+    contract(3)
+    back_1(3)
+    back_3(2)
+    back_2(3)
+    back_4(2)
+    back_3(3)
+    back_4(3)
+    total = held[z, c, own, :, features].astype(F32)
+    for k in range(1, spots):
+        back_line(k).wait_recv()
+        total = total + from_line[k - 1].astype(F32)
+    out_ref[...] = total.astype(BF16)
+    for k in range(1, spots):
+        to_line(k).wait_send()
+        back_line(k).wait_send()
+    for k in range(spots):
+        back_core(k).wait_send()
+        back_second(k, 0).wait_send()
+        back_second(k, 1).wait_send()
+        back_first(k).wait_send()
+
+
+def shards_fused(tokens, expert_ids, gate_values, expert_gate, expert_up, expert_down):
+    nodes = lax.axis_size("node")
+    per_node = lax.axis_size("local")
+    experts = nodes * per_node
+    spots = per_node // 2
+    tok_rows, width = tokens.shape
+    ff = expert_gate.shape[2]
+    cap = 2 * tok_rows * expert_ids.shape[1] // experts
+    dma = pltpu.SemaphoreType.DMA
+    vmem = pl.BlockSpec(memory_space=pltpu.VMEM)
+    anywhere = pl.BlockSpec(memory_space=pl.ANY)
+    wide = width + LANES
+    return pl.pallas_call(
+        functools.partial(fused, spots, experts, cap),
+        out_shape=jax.ShapeDtypeStruct((tok_rows, width), BF16),
+        in_specs=[anywhere, vmem, vmem, anywhere, anywhere, anywhere],
+        out_specs=vmem,
+        scratch_shapes=[
+            pltpu.VMEM((spots, 2, 4, tok_rows, wide), BF16),
+            pltpu.VMEM((tok_rows, wide), BF16),
+            pltpu.VMEM((spots, 4, tok_rows, width), BF16),
+            pltpu.VMEM((spots, 2, tok_rows, width), BF16),
+            pltpu.VMEM((spots, tok_rows, width), BF16),
+            pltpu.VMEM((spots - 1, tok_rows, width), BF16),
+            pltpu.VMEM((width, ff), BF16),
+            pltpu.VMEM((width, ff), BF16),
+            pltpu.VMEM((ff, width), BF16),
+            pltpu.VMEM((8 * cap, width), BF16),
+            pltpu.VMEM((8 * cap, ff), BF16),
+            pltpu.VMEM((2, 4 * tok_rows, 4 * cap), BF16),
+            pltpu.VMEM((2, 4 * tok_rows, 4 * cap), BF16),
+            dma((5,)),
+            dma((spots - 1,)),
+            dma((spots - 1,)),
+            dma((spots,)),
+            dma((spots,)),
+            dma((spots, 2)),
+            dma((spots, 2)),
+            dma((spots, 4)),
+            dma((spots, 4)),
+            dma((spots,)),
+            dma((spots,)),
+            dma((spots, 2)),
+            dma((spots, 2)),
+            dma((spots,)),
+            dma((spots,)),
+            dma((spots - 1,)),
+            dma((spots - 1,)),
+        ],
+        compiler_params=pltpu.CompilerParams(
+            collective_id=0, has_side_effects=True, vmem_limit_bytes=60 * 1024 * 1024
+        ),
+        cost_estimate=pl.CostEstimate(
+            flops=48 * experts * cap * width * ff // 8,
+            bytes_accessed=6 * width * ff,
+            transcendentals=experts * cap * ff,
+        ),
+    )(tokens, expert_ids, gate_values, expert_gate, expert_up, expert_down)
+
+
 def solution(mesh):
     placed = (
         P(("node", "local"), None),
@@ -75,6 +504,8 @@
         P(("node", "local"), None, None),
         P(("node", "local"), None, None),
     )
+    nodes, per_node = mesh.shape["node"], mesh.shape["local"]
+    shards = shards_fused if nodes == 4 and per_node == 8 else shards_all_to_all
     return jax.shard_map(
         shards, mesh=mesh, in_specs=placed, out_specs=P(("node", "local"), None), check_vma=False
     )

time: 378 us -> 178 us (0.47)
  Pallas kernels: 0 us -> 173 us
  blocking collectives: 170 us -> 0 us
  waiting for transfers between devices: 162 us -> 0 us
  matrix products: 36.7 us -> 0 us
    pallas_call x0 -> x1, Pallas kernels: none -> 173 us  [shards_fused(): pl.pallas_call(functools.partial(fused, spots, experts, cap), out_shape=j...]
    all_to_all x1 -> x0, blocking collectives: 170 us -> none  [shards(): lax.all_to_all(send.reshape(experts, cap, width), ('node', 'local'), spli...]
    all_to_all x1 -> x0, waiting for transfers between devices: 162 us -> none  [shards(): lax.all_to_all(expert_rows(lax.all_to_all(send.reshape(experts, cap, widt...]
    dot_general x5 -> x0, matrix products: 36.7 us -> none  [the longest x1 10.3 us: expert_rows(): gate_rows = jnp.dot(flat, w_gate, preferred_element_type=jnp.float32)]
  transfers between devices with their start and end apart: 1 -> 0, of which waited for: 1 -> 0; matrix products, arithmetic and copies ran while one was open for 0% -> 0% of each run, Pallas kernels for 0% -> 0%
where the time goes in v1:
time: 178 us
  Pallas kernels  173 us (97%)
  local copies, waits for them, and re-layouts  4.57 us (3%)
    pallas_call x1, Pallas kernels, shards_fused(): pl.pallas_call(functools.partial(fused, spots, experts, cap), out_shape=j...  173 us
    unnamed x3, local copies, waits for them, and re-layouts  4.57 us

profile of v1, /device:TPU:0, one launch (start us, length us, event | category | flops | bytes accessed | tf_op | source)
XLA Modules:
  0.0 177.7 jit_solution(17298328970924575302)
XLA Ops:
  0.0 1.4 copy.8.gates_ref
  1.4 1.4 copy.7.ids_ref
  2.8 173.1 %shard_map.64 = bf16[64,3584]{1,0:T(8,128)(2,1)} custom-call(bf16[64,3584]{1,0:T(8,128)(2,1)} %tok_ref.1, s32[64,8]{1,0:T(8,128)} %copy.7.ids_ref, bf16[64,8]{1,0:T(8,128)(2,1)} %copy.8.gates_ref, bf16[1,3584,1024]{2,1,0:T(8,128)(2,1)} %gate_hbm.1, bf16[1,3584,1024]{2,1,0:T(8,128)(2,1)} %up_hbm.1, bf16[1,1024,3584]{2,1,0:T(8,128)(2,1)} %down_hbm.1), custom_call_target="tpu_custom_call" | custom-call | flops 22548578304 | bytes 22020096 | tf_op jit(solution)/shard_map/pallas_call | solution.py:450
  175.9 1.8 %copy.10 = bf16[64,3584]{1,0:T(8,128)(2,1)} copy(bf16[64,3584]{1,0:T(8,128)(2,1)} %shard_map.64) | data formatting | bytes 917504

commit v2 on v1

--- a/solution.py
+++ b/solution.py
@@ -74,6 +74,92 @@
     return jnp.sum(node_part.astype(jnp.float32), axis=0).astype(jnp.bfloat16)
 
 
+PLAN = (
+    ("ga", 0, 0),
+    ("gb", 0, 0),
+    ("zz", 2, 0),
+    ("ga", 1, 0),
+    ("gc", 0, 0),
+    ("gc", 0, 1),
+    ("gd", 0, 0),
+    ("zz", 3, 0),
+    ("D", 0, 0),
+    ("E", 0, 0),
+    ("E", 0, 1),
+    ("E", 0, 2),
+    ("E", 0, 3),
+    ("C", 0, 0),
+    ("gc", 1, 0),
+    ("gb", 1, 0),
+    ("ga", 2, 0),
+    ("C", 0, 1),
+    ("gb", 2, 0),
+    ("gc", 1, 1),
+    ("b2", 0, 0),
+    ("gd", 1, 0),
+    ("D", 1, 0),
+    ("E", 1, 0),
+    ("E", 1, 1),
+    ("gc", 2, 1),
+    ("ga", 3, 0),
+    ("E", 1, 2),
+    ("E", 1, 3),
+    ("gc", 2, 0),
+    ("C", 1, 0),
+    ("b2", 0, 1),
+    ("gb", 3, 0),
+    ("C", 1, 1),
+    ("gd", 2, 0),
+    ("gc", 3, 0),
+    ("D", 2, 0),
+    ("b2", 1, 0),
+    ("E", 2, 0),
+    ("b2", 1, 1),
+    ("E", 2, 1),
+    ("E", 2, 2),
+    ("b3", 1, 0),
+    ("bq", 0, 0),
+    ("E", 2, 3),
+    ("gc", 3, 1),
+    ("b3", 1, 1),
+    ("bq", 0, 1),
+    ("C", 2, 0),
+    ("C", 2, 1),
+    ("gd", 3, 0),
+    ("b3", 0, 0),
+    ("b4", 1, 1),
+    ("D", 3, 0),
+    ("b3", 0, 1),
+    ("b2", 2, 0),
+    ("b4", 0, 0),
+    ("b4", 1, 0),
+    ("E", 3, 0),
+    ("b2", 2, 1),
+    ("E", 3, 1),
+    ("E", 3, 2),
+    ("b3", 2, 0),
+    ("E", 3, 3),
+    ("C", 3, 0),
+    ("b3", 2, 1),
+    ("b4", 2, 0),
+    ("b2", 3, 0),
+    ("b4", 2, 1),
+    ("C", 3, 1),
+    ("b3", 3, 0),
+    ("b4", 0, 1),
+    ("b2", 3, 1),
+    ("b3", 3, 1),
+    ("b4", 3, 0),
+    ("b4", 3, 1),
+)
+
+
+def column_parts(width):
+    tiles = width // 512
+    lead = (tiles + 1) // 2 * 512
+    return ((0, lead), (lead, width - lead))
+
+
 def fused(
     spots,
     experts,
@@ -87,10 +173,12 @@
     out_ref,
     held,
     mine,
+    spare,
     from_core,
     from_second,
     from_first,
     from_line,
+    from_corner,
     w_gate,
     w_up,
     w_down,
@@ -115,10 +203,15 @@
     back_first_r,
     back_line_s,
     back_line_r,
+    corner_s,
+    corner_r,
+    back_corner_s,
+    back_corner_r,
 ):
     tok_rows, width = tok_ref.shape
     ff = w_gate.shape[1]
     quad = 4 * tok_rows
+    columns = column_parts(width)
     slots = 4 * cap
     node = lax.axis_index("node")
     local = lax.axis_index("local")
@@ -133,7 +226,7 @@
     def q_core(i, j):
         return i * step_b + j * step_a
 
-    own = q(a, b)
+    own, far = q(a, b), q(1 - a, 1 - b)
     order = ((a, b), (1 - a, b), (a, 1 - b), (1 - a, 1 - b))
     order_core = ((b, a), (1 - b, a), (b, 1 - a), (1 - b, 1 - a))
     first = ((y + c * (1 - 2 * y)) * 2 + c, z * 2 + x + (1 - c) * (1 - 2 * x))
@@ -162,22 +255,23 @@
     for load in loads:
         load.start()
 
-    lane = lax.broadcasted_iota(jnp.int32, (tok_rows, LANES), 1)
-    weight = jnp.zeros((tok_rows, LANES), F32)
-    hit = jnp.zeros((tok_rows, LANES), F32)
-    for k in range(ids_ref.shape[1]):
-        chosen = ids_ref[:, k : k + 1]
-        value = gates_ref[:, k : k + 1].astype(F32)
+    lane = lax.broadcasted_iota(jnp.int32, (LANES, tok_rows), 0)
+    weight = jnp.zeros((LANES, tok_rows), F32)
+    hit = jnp.zeros((LANES, tok_rows), F32)
+    for k in range(ids_ref.shape[0]):
+        chosen = ids_ref[k : k + 1, :]
+        value = gates_ref[k : k + 1, :].astype(F32)
         weight = weight + jnp.where(lane == chosen, value, 0.0)
         hit = hit + jnp.where(lane == chosen + experts, 1.0, 0.0)
     earlier = (
         lax.broadcasted_iota(jnp.int32, (tok_rows, tok_rows), 0)
-        > lax.broadcasted_iota(jnp.int32, (tok_rows, tok_rows), 1)
+        < lax.broadcasted_iota(jnp.int32, (tok_rows, tok_rows), 1)
     )
     before = jnp.dot(
-        jnp.where(earlier, 1.0, 0.0).astype(BF16), hit.astype(BF16), preferred_element_type=F32
+        hit.astype(BF16), jnp.where(earlier, 1.0, 0.0).astype(BF16), preferred_element_type=F32
     )
-    mine[:, pl.ds(width, LANES)] = (weight + hit * (before + 1.0)).astype(BF16)
+    notes = jnp.transpose(weight + hit * (before + 1.0))
+    mine[:, pl.ds(width, LANES)] = notes.astype(BF16)
     loads[0].wait()
     keep = pltpu.make_async_copy(mine, held.at[z, c, own], local_sem.at[4])
     keep.start()
@@ -218,20 +312,30 @@
         to_second(k, 0).start()
         to_core(k, 0).start()
         if k == 0:
-            for hop in range(1, spots):
-                to_line(hop).start()
+            to_line(1).start()
 
     def gather_b(k):
         send(mine, block(k, 1), first_s.at[k], first_r.at[k], first).wait_recv()
-        to_second(k, 1).start()
+        if k != 1:
+            to_second(k, 1).start()
         to_core(k, 1).start()
 
-    def gather_c(k):
-        for i in range(2):
+    def corner():
+        return send(spare, held.at[z, c, far], corner_s.at[0], corner_r.at[0], along(1))
+
+    def gather_c(k, i):
+        if k == 1 and i == 1:
+            send(spare, block(1, 3), corner_s.at[0], corner_r.at[0], along(1)).wait_recv()
+        else:
             send(
                 mine, block(k, 2 + i), second_s.at[k, i], second_r.at[k, i], second
             ).wait_recv()
-            to_core(k, 2 + i).start()
+        to_core(k, 2 + i).start()
+        if k == 0 and i == 1:
+            copy = pltpu.make_async_copy(block(0, 3), spare, local_sem.at[5])
+            copy.start()
+            copy.wait()
+            corner().start()
 
     def gather_d(k):
         for i in range(4):
@@ -240,7 +344,7 @@
 
     def gather_sent(k):
         to_first(k).wait_send()
-        for i in range(2):
+        for i in range(1 if k == 1 else 2):
             to_second(k, i).wait_send()
         for i in range(4):
             to_core(k, i).wait_send()
@@ -257,41 +361,38 @@
                 jnp.where(lane == expert + experts, notes, 0.0), axis=1, keepdims=True
             )
             target = jnp.where(place > 0.0, place - 1.0 + base, -1.0)
-            pick[h] = jnp.where(column == target, 1.0, 0.0).astype(BF16)
+            pick[h] = jnp.transpose(jnp.where(column == target, 1.0, 0.0)).astype(BF16)
             blend[h] = jnp.where(column == target, weight, 0.0).astype(BF16)
 
         def piece(j, carry):
             cols = pl.ds(pl.multiple_of(j * 512, 512), 512)
             for h in range(2):
-                rows[pl.ds(h * slots, slots), cols] = lax.dot_general(
+                rows[pl.ds(h * slots, slots), cols] = jnp.dot(
                     pick[h],
                     held[s, h, :, :, cols].reshape(quad, 512),
-                    (((0,), (0,)), ((), ())),
                     preferred_element_type=F32,
                 ).astype(BF16)
             return carry
 
         lax.fori_loop(0, width // 512, piece, 0)
 
-    def expand(k):
-        if k == 0:
+    def expand(k, part):
+        if k == 0 and part == 0:
             loads[1].wait()
             loads[2].wait()
 
-        def piece(j, carry):
-            cols = pl.ds(pl.multiple_of(j * 256, 256), 256)
-            gate = jnp.dot(rows[...], w_gate[:, cols], preferred_element_type=F32)
-            up = jnp.dot(rows[...], w_up[:, cols], preferred_element_type=F32)
-            hidden[:, cols] = (gate / (1.0 + jnp.exp(-gate)) * up).astype(BF16)
-            return carry
-
-        lax.fori_loop(0, ff // 256, piece, 0)
-
-    def contract(k):
+        tile = ff // 4
+        cols = pl.ds(part * tile, tile)
+        gate = jnp.dot(rows[...], w_gate[:, cols], preferred_element_type=F32)
+        up = jnp.dot(rows[...], w_up[:, cols], preferred_element_type=F32)
+        hidden[:, cols] = (gate / (1.0 + jnp.exp(-gate)) * up).astype(BF16)
+
+    def contract(k, part):
         s = spot(k)
-        if k == 0:
-            loads[3].wait()
-        gather_sent(k)
+        if part == 0:
+            if k == 0:
+                loads[3].wait()
+            gather_sent(k)
 
         def piece(j, carry):
             cols = pl.ds(pl.multiple_of(j * 512, 512), 512)
@@ -306,133 +407,136 @@
                 )
             return carry
 
-        lax.fori_loop(0, width // 512, piece, 0)
-
-    features = pl.ds(0, width)
-
-    def back_core(k):
+        start, size = columns[part]
+        lax.fori_loop(start // 512, (start + size) // 512, piece, 0)
+        back_core(k, part).start()
+
+    def span(part):
+        start, size = columns[part]
+        return pl.ds(start, size)
+
+    def back_core(k, part):
         return send(
-            held.at[spot(k), 1 - c, :, :, features],
-            from_core.at[k],
-            back_core_s.at[k],
-            back_core_r.at[k],
+            held.at[spot(k), 1 - c, :, :, span(part)],
+            from_core.at[k, :, :, span(part)],
+            back_core_s.at[k, part],
+            back_core_r.at[k, part],
             sibling,
         )
 
-    def back_second(k, i):
+    def back_second(k, i, part):
         return send(
-            held.at[spot(k), c, q(i, 1 - b), :, features],
-            from_second.at[k, i],
-            back_second_s.at[k, i],
-            back_second_r.at[k, i],
+            held.at[spot(k), c, q(*order[2 + i]), :, span(part)],
+            from_second.at[k, i, :, span(part)],
+            back_second_s.at[k, i, part],
+            back_second_r.at[k, i, part],
             second,
         )
 
-    def back_first(k):
+    def back_corner(part):
         return send(
-            held.at[spot(k), c, q(1 - a, b), :, features],
-            from_first.at[k],
-            back_first_s.at[k],
-            back_first_r.at[k],
+            held.at[spot(1), c, far, :, span(part)],
+            from_corner.at[:, span(part)],
+            back_corner_s.at[part],
+            back_corner_r.at[part],
+            (node, spot(1) * 2 + x),
+        )
+
+    def back_first(k, part):
+        return send(
+            held.at[spot(k), c, q(1 - a, b), :, span(part)],
+            from_first.at[k, :, span(part)],
+            back_first_s.at[k, part],
+            back_first_r.at[k, part],
             first,
         )
 
-    def back_line(k):
+    def back_line(k, part):
         return send(
-            held.at[spot(k), c, own, :, features],
-            from_line.at[k - 1],
-            back_line_s.at[k - 1],
-            back_line_r.at[k - 1],
+            held.at[spot(k), c, own, :, span(part)],
+            from_line.at[k - 1, :, span(part)],
+            back_line_s.at[k - 1, part],
+            back_line_r.at[k - 1, part],
             (node, spot(k) * 2 + x),
         )
 
-    def add(k, place, other):
-        held[spot(k), c, place, :, features] = (
-            held[spot(k), c, place, :, features].astype(F32) + other.astype(F32)
+    def add(k, place, part, other):
+        cols = span(part)
+        held[spot(k), c, place, :, cols] = (
+            held[spot(k), c, place, :, cols].astype(F32) + other.astype(F32)
         ).astype(BF16)
 
-    def back_1(k):
-        back_core(k).start()
-
-    def back_2(k):
-        back_core(k).wait_recv()
-        for i in range(2):
-            add(k, q(i, 1 - b), from_core[k, q(i, 1 - b)])
-            back_second(k, i).start()
-        for i in range(2):
-            add(k, q(i, b), from_core[k, q(i, b)])
-
-    def back_3(k):
-        back_second(k, 0).wait_recv()
-        back_second(k, 1).wait_recv()
-        add(k, q(1 - a, b), from_second[k, 1 - a])
-        back_first(k).start()
-        add(k, own, from_second[k, a])
-
-    def back_4(k):
-        back_first(k).wait_recv()
-        add(k, own, from_first[k])
+    def back_2(k, part):
+        cols = span(part)
+        back_core(k, part).wait_recv()
+        add(k, q(a, 1 - b), part, from_core[k, q(a, 1 - b), :, cols])
+        back_second(k, 0, part).start()
+        add(k, far, part, from_core[k, far, :, cols])
+        if k == 1:
+            back_corner(part).start()
+        elif k > 1:
+            back_second(k, 1, part).start()
+        add(k, q(1 - a, b), part, from_core[k, q(1 - a, b), :, cols])
+        add(k, own, part, from_core[k, own, :, cols])
+
+    def back_far(part):
+        back_corner(part).wait_recv()
+        add(0, far, part, from_corner[:, span(part)])
+        back_second(0, 1, part).start()
+
+    def back_3(k, part):
+        cols = span(part)
+        back_second(k, 0, part).wait_recv()
+        if k != 1:
+            back_second(k, 1, part).wait_recv()
+            add(k, q(1 - a, b), part, from_second[k, 1, :, cols])
+        back_first(k, part).start()
+        add(k, own, part, from_second[k, 0, :, cols])
+
+    def back_4(k, part):
+        back_first(k, part).wait_recv()
+        add(k, own, part, from_first[k, :, span(part)])
         if k > 0:
-            back_line(k).start()
-
-    gather_a(0)
-    gather_b(0)
-    gather_a(1)
-    gather_c(0)
-    gather_b(1)
-    gather_d(0)
-    keep.wait()
-    dispatch(0)
-    expand(0)
-    gather_c(1)
-    gather_a(2)
-    contract(0)
-    back_1(0)
-    gather_b(2)
-    gather_d(1)
-    dispatch(1)
-    back_2(0)
-    expand(1)
-    gather_c(2)
-    gather_a(3)
-    contract(1)
-    back_1(1)
-    back_3(0)
-    gather_b(3)
-    gather_d(2)
-    dispatch(2)
-    back_2(1)
-    expand(2)
-    gather_c(3)
-    back_4(0)
-    contract(2)
-    back_1(2)
-    back_3(1)
-    gather_d(3)
-    dispatch(3)
-    back_2(2)
-    expand(3)
-    back_4(1)
-    contract(3)
-    back_1(3)
-    back_3(2)
-    back_2(3)
-    back_4(2)
-    back_3(3)
-    back_4(3)
-    total = held[z, c, own, :, features].astype(F32)
-    for k in range(1, spots):
-        back_line(k).wait_recv()
-        total = total + from_line[k - 1].astype(F32)
-    out_ref[...] = total.astype(BF16)
+            back_line(k, part).start()
+
+    steps = {
+        "ga": lambda k, i: gather_a(k),
+        "zz": lambda k, i: to_line(k).start(),
+        "gb": lambda k, i: gather_b(k),
+        "gc": gather_c,
+        "gd": lambda k, i: gather_d(k),
+        "D": lambda k, i: dispatch(k),
+        "E": expand,
+        "C": contract,
+        "b2": back_2,
+        "bq": lambda k, i: back_far(i),
+        "b3": back_3,
+        "b4": back_4,
+    }
+    for name, k, i in PLAN:
+        if name == "D" and k == 0:
+            keep.wait()
+        steps[name](k, i)
+    for part in range(len(columns)):
+        cols = span(part)
+        total = held[z, c, own, :, cols].astype(F32)
+        for k in range(1, spots):
+            back_line(k, part).wait_recv()
+            total = total + from_line[k - 1, :, cols].astype(F32)
+        out_ref[:, cols] = total.astype(BF16)
     for k in range(1, spots):
         to_line(k).wait_send()
-        back_line(k).wait_send()
-    for k in range(spots):
-        back_core(k).wait_send()
-        back_second(k, 0).wait_send()
-        back_second(k, 1).wait_send()
-        back_first(k).wait_send()
+    corner().wait_send()
+    for part in range(len(columns)):
+        back_corner(part).wait_send()
+        for k in range(spots):
+            back_core(k, part).wait_send()
+            back_first(k, part).wait_send()
+            back_second(k, 0, part).wait_send()
+            if k != 1:
+                back_second(k, 1, part).wait_send()
+            if k > 0:
+                back_line(k, part).wait_send()
 
 
 def shards_fused(tokens, expert_ids, gate_values, expert_gate, expert_up, expert_down):
@@ -444,6 +548,7 @@
     ff = expert_gate.shape[2]
     cap = 2 * tok_rows * expert_ids.shape[1] // experts
     dma = pltpu.SemaphoreType.DMA
+    parts = len(column_parts(width))
     vmem = pl.BlockSpec(memory_space=pltpu.VMEM)
     anywhere = pl.BlockSpec(memory_space=pl.ANY)
     wide = width + LANES
@@ -455,18 +560,20 @@
         scratch_shapes=[
             pltpu.VMEM((spots, 2, 4, tok_rows, wide), BF16),
             pltpu.VMEM((tok_rows, wide), BF16),
+            pltpu.VMEM((tok_rows, wide), BF16),
             pltpu.VMEM((spots, 4, tok_rows, width), BF16),
             pltpu.VMEM((spots, 2, tok_rows, width), BF16),
             pltpu.VMEM((spots, tok_rows, width), BF16),
             pltpu.VMEM((spots - 1, tok_rows, width), BF16),
+            pltpu.VMEM((tok_rows, width), BF16),
             pltpu.VMEM((width, ff), BF16),
             pltpu.VMEM((width, ff), BF16),
             pltpu.VMEM((ff, width), BF16),
             pltpu.VMEM((8 * cap, width), BF16),
             pltpu.VMEM((8 * cap, ff), BF16),
+            pltpu.VMEM((2, 4 * cap, 4 * tok_rows), BF16),
             pltpu.VMEM((2, 4 * tok_rows, 4 * cap), BF16),
-            pltpu.VMEM((2, 4 * tok_rows, 4 * cap), BF16),
-            dma((5,)),
+            dma((6,)),
             dma((spots - 1,)),
             dma((spots - 1,)),
             dma((spots,)),
@@ -475,14 +582,18 @@
             dma((spots, 2)),
             dma((spots, 4)),
             dma((spots, 4)),
-            dma((spots,)),
-            dma((spots,)),
-            dma((spots, 2)),
-            dma((spots, 2)),
-            dma((spots,)),
-            dma((spots,)),
-            dma((spots - 1,)),
-            dma((spots - 1,)),
+            dma((spots, parts)),
+            dma((spots, parts)),
+            dma((spots, 2, parts)),
+            dma((spots, 2, parts)),
+            dma((spots, parts)),
+            dma((spots, parts)),
+            dma((spots - 1, parts)),
+            dma((spots - 1, parts)),
+            dma((1,)),
+            dma((1,)),
+            dma((parts,)),
+            dma((parts,)),
         ],
         compiler_params=pltpu.CompilerParams(
             collective_id=0, has_side_effects=True, vmem_limit_bytes=60 * 1024 * 1024
@@ -492,7 +603,7 @@
             bytes_accessed=6 * width * ff,
             transcendentals=experts * cap * ff,
         ),
-    )(tokens, expert_ids, gate_values, expert_gate, expert_up, expert_down)
+    )(tokens, expert_ids.T, gate_values.T, expert_gate, expert_up, expert_down)
 
 
 def solution(mesh):

time: 178 us -> 160 us (0.90)
  Pallas kernels: 173 us -> 158 us
  local copies, waits for them, and re-layouts: 4.57 us -> 1.82 us
    pallas_call x1, Pallas kernels: 173 us -> 158 us  [shards_fused(): pl.pallas_call(functools.partial(fused, spots, experts, cap), out_shape=j...]
    unnamed x3 -> x1, local copies, waits for them, and re-layouts: 4.57 us -> 1.82 us
where the time goes in v2:
time: 160 us
  Pallas kernels  158 us (99%)
  local copies, waits for them, and re-layouts  1.82 us (1%)
    pallas_call x1, Pallas kernels, shards_fused(): pl.pallas_call(functools.partial(fused, spots, experts, cap), out_shape=j...  158 us

profile of v2, /device:TPU:0, one launch (start us, length us, event | category | flops | bytes accessed | tf_op | source)
XLA Modules:
  0.0 159.6 jit_solution(15795655026105635171)
XLA Ops:
  0.0 157.8 %shard_map.64 = bf16[64,3584]{1,0:T(8,128)(2,1)} custom-call(bf16[64,3584]{1,0:T(8,128)(2,1)} %tok_ref.1, s32[8,64]{1,0:T(8,128)} %bitcast.2, bf16[8,64]{1,0:T(8,128)(2,1)} %bitcast.3, bf16[1,3584,1024]{2,1,0:T(8,128)(2,1)} %gate_hbm.1, bf16[1,3584,1024]{2,1,0:T(8,128)(2,1)} %up_hbm.1, bf16[1,1024,3584]{2,1,0:T(8,128)(2,1)} %down_hbm.1), custom_call_target="tpu_custom_call" | custom-call | flops 22548578304 | bytes 22020096 | tf_op jit(solution)/shard_map/pallas_call | solution.py:555
  157.8 1.8 %copy.8 = bf16[64,3584]{1,0:T(8,128)(2,1)} copy(bf16[64,3584]{1,0:T(8,128)(2,1)} %shard_map.64) | data formatting | bytes 917504

commit v3 on v2

--- a/solution.py
+++ b/solution.py
@@ -76,81 +76,73 @@
 
 PLAN = (
     ("ga", 0, 0),
+    ("zz", 2, 0),
     ("gb", 0, 0),
-    ("zz", 2, 0),
     ("ga", 1, 0),
     ("gc", 0, 0),
     ("gc", 0, 1),
+    ("zz", 3, 0),
     ("gd", 0, 0),
-    ("zz", 3, 0),
     ("D", 0, 0),
     ("E", 0, 0),
     ("E", 0, 1),
-    ("E", 0, 2),
-    ("E", 0, 3),
     ("C", 0, 0),
+    ("ga", 2, 0),
+    ("C", 0, 1),
     ("gc", 1, 0),
     ("gb", 1, 0),
-    ("ga", 2, 0),
-    ("C", 0, 1),
+    ("gc", 1, 1),
     ("gb", 2, 0),
-    ("gc", 1, 1),
+    ("b2", 0, 1),
     ("b2", 0, 0),
     ("gd", 1, 0),
     ("D", 1, 0),
+    ("gc", 2, 0),
     ("E", 1, 0),
+    ("gc", 2, 1),
     ("E", 1, 1),
-    ("gc", 2, 1),
     ("ga", 3, 0),
-    ("E", 1, 2),
-    ("E", 1, 3),
-    ("gc", 2, 0),
     ("C", 1, 0),
-    ("b2", 0, 1),
+    ("gd", 2, 0),
+    ("C", 1, 1),
+    ("b2", 1, 0),
+    ("D", 2, 0),
+    ("E", 2, 0),
     ("gb", 3, 0),
-    ("C", 1, 1),
-    ("gd", 2, 0),
-    ("gc", 3, 0),
-    ("D", 2, 0),
-    ("b2", 1, 0),
-    ("E", 2, 0),
+    ("bq", 0, 0),
     ("b2", 1, 1),
     ("E", 2, 1),
-    ("E", 2, 2),
     ("b3", 1, 0),
-    ("bq", 0, 0),
-    ("E", 2, 3),
+    ("gc", 3, 0),
     ("gc", 3, 1),
-    ("b3", 1, 1),
-    ("bq", 0, 1),
     ("C", 2, 0),
     ("C", 2, 1),
+    ("b3", 1, 1),
     ("gd", 3, 0),
+    ("D", 3, 0),
+    ("b2", 2, 0),
+    ("b2", 2, 1),
+    ("b4", 1, 0),
+    ("b4", 1, 1),
+    ("E", 3, 0),
+    ("b3", 2, 0),
+    ("E", 3, 1),
+    ("b3", 2, 1),
     ("b3", 0, 0),
-    ("b4", 1, 1),
-    ("D", 3, 0),
-    ("b3", 0, 1),
-    ("b2", 2, 0),
-    ("b4", 0, 0),
-    ("b4", 1, 0),
-    ("E", 3, 0),
-    ("b2", 2, 1),
-    ("E", 3, 1),
-    ("E", 3, 2),
-    ("b3", 2, 0),
-    ("E", 3, 3),
+    ("bq", 0, 1),
+    ("b4", 2, 0),
     ("C", 3, 0),
-    ("b3", 2, 1),
-    ("b4", 2, 0),
+    ("C", 3, 1),
     ("b2", 3, 0),
     ("b4", 2, 1),
-    ("C", 3, 1),
     ("b3", 3, 0),
+    ("b2", 3, 1),
+    ("b4", 3, 0),
+    ("b3", 0, 1),
+    ("b3", 3, 1),
     ("b4", 0, 1),
-    ("b2", 3, 1),
-    ("b3", 3, 1),
-    ("b4", 3, 0),
     ("b4", 3, 1),
+    ("b4", 0, 0),
 )
 
 
@@ -364,24 +356,21 @@
             pick[h] = jnp.transpose(jnp.where(column == target, 1.0, 0.0)).astype(BF16)
             blend[h] = jnp.where(column == target, weight, 0.0).astype(BF16)
 
-        def piece(j, carry):
-            cols = pl.ds(pl.multiple_of(j * 512, 512), 512)
+        for j in range(width // 512):
+            cols = pl.ds(j * 512, 512)
             for h in range(2):
                 rows[pl.ds(h * slots, slots), cols] = jnp.dot(
                     pick[h],
                     held[s, h, :, :, cols].reshape(quad, 512),
                     preferred_element_type=F32,
                 ).astype(BF16)
-            return carry
-
-        lax.fori_loop(0, width // 512, piece, 0)
 
     def expand(k, part):
         if k == 0 and part == 0:
             loads[1].wait()
             loads[2].wait()
 
-        tile = ff // 4
+        tile = ff // 2
         cols = pl.ds(part * tile, tile)
         gate = jnp.dot(rows[...], w_gate[:, cols], preferred_element_type=F32)
         up = jnp.dot(rows[...], w_up[:, cols], preferred_element_type=F32)
@@ -394,8 +383,9 @@
                 loads[3].wait()
             gather_sent(k)
 
-        def piece(j, carry):
-            cols = pl.ds(pl.multiple_of(j * 512, 512), 512)
+        start, size = columns[part]
+        for j in range(start // 512, (start + size) // 512):
+            cols = pl.ds(j * 512, 512)
             made = jnp.dot(hidden[...], w_down[:, cols], preferred_element_type=F32).astype(BF16)
             for h in range(2):
                 held[s, h, :, :, cols] = (
@@ -405,10 +395,6 @@
                     .astype(BF16)
                     .reshape(4, tok_rows, 512)
                 )
-            return carry
-
-        start, size = columns[part]
-        lax.fori_loop(start // 512, (start + size) // 512, piece, 0)
         back_core(k, part).start()
 
     def span(part):

time: 160 us -> 155 us (0.969)
  Pallas kernels: 158 us -> 153 us
    pallas_call x1, Pallas kernels: 158 us -> 153 us  [shards_fused(): pl.pallas_call(functools.partial(fused, spots, experts, cap), out_shape=j...]
where the time goes in v3:
time: 155 us
  Pallas kernels  153 us (99%)
  local copies, waits for them, and re-layouts  1.82 us (1%)
    pallas_call x1, Pallas kernels, shards_fused(): pl.pallas_call(functools.partial(fused, spots, experts, cap), out_shape=j...  153 us

profile of v3, /device:TPU:0, one launch (start us, length us, event | category | flops | bytes accessed | tf_op | source)
XLA Modules:
  0.0 154.9 jit_solution(7832677763226908199)
XLA Ops:
  0.0 153.1 %shard_map.64 = bf16[64,3584]{1,0:T(8,128)(2,1)} custom-call(bf16[64,3584]{1,0:T(8,128)(2,1)} %tok_ref.1, s32[8,64]{1,0:T(8,128)} %bitcast.2, bf16[8,64]{1,0:T(8,128)(2,1)} %bitcast.3, bf16[1,3584,1024]{2,1,0:T(8,128)(2,1)} %gate_hbm.1, bf16[1,3584,1024]{2,1,0:T(8,128)(2,1)} %up_hbm.1, bf16[1,1024,3584]{2,1,0:T(8,128)(2,1)} %down_hbm.1), custom_call_target="tpu_custom_call" | custom-call | flops 22548578304 | bytes 22020096 | tf_op jit(solution)/shard_map/pallas_call | solution.py:541
  153.1 1.8 %copy.8 = bf16[64,3584]{1,0:T(8,128)(2,1)} copy(bf16[64,3584]{1,0:T(8,128)(2,1)} %shard_map.64) | data formatting | bytes 917504
